TPU v7x, 32 devices: a whole 2x2x4 slice. The times are simulated.
32 devices in a mesh: replica: 2 (over x), pool: 16 (over z, y, core).
Axes of the slice: x: 2, y: 2, z: 4, core: 2. Of those that a mesh axis runs over, the one named last changes fastest.
Arguments:
- stretch_queries: bfloat16 [4096, 8192], P(('replica', 'pool')), parts along dimension 0, may hold values from -7 to 7
- decode_queries: bfloat16 [128, 8192], P(('replica', 'pool')), parts along dimension 0, may hold values from -7 to 7
- stretch_entries: bfloat16 [2, 4096, 1024], P(None, ('replica', 'pool')), parts along dimension 1, may hold values from -7 to 7
- decode_entries: bfloat16 [2, 128, 1024], P(None, ('replica', 'pool')), parts along dimension 1, may hold values from -7 to 7
- pool_pages: bfloat16 [2048, 2, 16, 1024], P(('replica', 'pool')), parts along dimension 0, may hold values from -7 to 7
- page_owner: int32 [3072, 1], P(('replica', 'pool')), parts along dimension 0, may hold values from 0 to 15; in each aligned block of 96 rows (0 to 95, 96 to 191, ...) at most 8 rows name the same one
- page_slot: int32 [3072], P(('replica', 'pool')), parts along dimension 0, may hold values from 0 to 63
- prefix_length: int32 [32], P(('replica', 'pool')), parts along dimension 0, may hold values from 0 to 768, as said below
- context_length: int32 [128], P(('replica', 'pool')), parts along dimension 0, may hold values from 1 to 192, as said below
Outputs:
- stretch_output: bfloat16 [4096, 8192], P(('replica', 'pool')), parts along dimension 0
- decode_output: bfloat16 [128, 8192], P(('replica', 'pool')), parts along dimension 0
There are 2 independent parts, one for each index of `replica`. A program takes and returns all parts, laid end to end along the dimension named above; each array names one. Nothing has to cross between parts.
Inputs may be any that keep to these rules, and one draw needn't show every extreme that they name: `page_owner`: in the 96 rows of one device no owner appears more than 8 times; in some devices' rows one owner appears exactly 8 times. `prefix_length`: some batch shard has the full 48 * 16 prefix positions. `context_length`: some decode row has the full 12 * 16 positions.
All inputs are finite; a program needn't handle non-finite values.
Results may differ from a plain program's by a relative error of at most 0.0046.
Values may be sent and summed in bfloat16 or wider, within the bound.
A program may use at most 192 MiB of HBM per device.

v0:
```python
import functools
import math

import jax
import jax.numpy as jnp
from jax import lax
from jax.experimental import pallas as pl
from jax.experimental.pallas import tpu as pltpu
from jax.sharding import PartitionSpec as P

HEADS = 64
HEAD_DIM = 128
PRE_PAGES = 48
DEC_PAGES = 12
LOG2_SCALE = math.log2(math.e) / math.sqrt(HEAD_DIM)
PLANE = 4
MESH = pl.DeviceIdType.MESH
CONTRACT_LAST = (((1,), (1,)), ((), ()))


def scores_of(queries, keys):
    return lax.dot_general(queries, keys, CONTRACT_LAST, preferred_element_type=jnp.float32)


def weigh(score_parts, value_parts):
    highest = functools.reduce(
        jnp.maximum, [jnp.max(s, axis=1, keepdims=True) for s in score_parts]
    )
    total = 0.0
    summed = 0.0
    for scores, values in zip(score_parts, value_parts):
        terms = jnp.exp2((scores - highest) * LOG2_SCALE)
        total = total + jnp.sum(terms, axis=1, keepdims=True)
        summed = summed + jnp.dot(
            terms.astype(jnp.bfloat16), values, preferred_element_type=jnp.float32
        )
    return summed / total


def attention_kernel(
    places, prefix_length, context_length,
    queries, decode_queries, entries, decode_entries, pages, own_pages,
    output, decode_output, cache, sem,
):
    page_count, _, page_tokens, _ = cache.shape
    head = pl.program_id(0)
    row_count = queries.shape[0]
    group = queries.shape[1] // HEAD_DIM

    @pl.when(head == 0)
    def _():
        def fetch(t, carry):
            place = places[t]

            @pl.when(place >= 0)
            def _():
                pltpu.make_async_copy(pages.at[place], cache.at[t], sem).start()

            @pl.when(place < 0)
            def _():
                pltpu.make_async_copy(own_pages.at[-1 - place], cache.at[t], sem).start()

            return carry

        lax.fori_loop(0, page_count, fetch, 0)
        pltpu.make_async_copy(cache, cache, sem).wait()

    columns = pl.ds(pl.multiple_of(head * HEAD_DIM, HEAD_DIM), HEAD_DIM)
    span = PRE_PAGES * page_tokens
    prefix_keys = cache[:PRE_PAGES, 0, :, columns].reshape(span, HEAD_DIM)
    prefix_values = cache[:PRE_PAGES, 1, :, columns].reshape(span, HEAD_DIM)
    position = lax.broadcasted_iota(jnp.int32, (1, span), 1)
    prefix_bias = jnp.where(position < prefix_length[0], 0.0, -jnp.inf)
    causal_bias = jnp.where(
        lax.broadcasted_iota(jnp.int32, (row_count, row_count), 0)
        >= lax.broadcasted_iota(jnp.int32, (row_count, row_count), 1),
        0.0,
        -jnp.inf,
    )
    own_keys = entries[0]
    own_values = entries[1]
    step = 4
    for start in range(0, group, step):
        stacked = jnp.concatenate(
            [queries[:, g * HEAD_DIM : (g + 1) * HEAD_DIM] for g in range(start, start + step)],
            axis=0,
        )
        own_scores = scores_of(stacked, own_keys).reshape(step, row_count, row_count)
        own_scores = (own_scores + causal_bias[None]).reshape(step * row_count, row_count)
        prefix_scores = scores_of(stacked, prefix_keys) + prefix_bias
        result = weigh([own_scores, prefix_scores], [own_values, prefix_values])
        result = result.astype(jnp.bfloat16)
        for g in range(step):
            output[:, (start + g) * HEAD_DIM : (start + g + 1) * HEAD_DIM] = result[
                g * row_count : (g + 1) * row_count
            ]

    context_span = (page_count - PRE_PAGES) * page_tokens
    row_span = DEC_PAGES * page_tokens
    context_keys = cache[PRE_PAGES:, 0, :, columns].reshape(context_span, HEAD_DIM)
    context_values = cache[PRE_PAGES:, 1, :, columns].reshape(context_span, HEAD_DIM)
    row_queries = decode_queries[0]
    shape = (row_queries.shape[0], context_span)
    row = lax.broadcasted_iota(jnp.int32, shape, 0) // group
    place = lax.broadcasted_iota(jnp.int32, shape, 1)
    usable = jnp.zeros(shape, jnp.bool_)
    for r in range(context_span // row_span):
        usable = usable | (
            (row == r) & (place >= r * row_span) & (place < r * row_span + context_length[r])
        )
    context_scores = jnp.where(usable, scores_of(row_queries, context_keys), -jnp.inf)
    new_scores = scores_of(row_queries, decode_entries[0])
    own = lax.broadcasted_iota(jnp.int32, new_scores.shape, 0) // group
    own = own == lax.broadcasted_iota(jnp.int32, new_scores.shape, 1)
    new_scores = jnp.where(own, new_scores, -jnp.inf)
    decode_output[0] = weigh(
        [new_scores, context_scores], [decode_entries[1], context_values]
    ).astype(jnp.bfloat16)


def attention(places, prefix_length, context_length, queries, decode_queries, entries,
              decode_entries, pages, own_pages):
    row_count = queries.shape[0]
    decode_count = decode_queries.shape[0]
    key_heads = pages.shape[-1] // HEAD_DIM
    group = HEADS // key_heads
    page_count = places.shape[0]
    arranged = decode_queries.reshape(decode_count, key_heads, group, HEAD_DIM)
    arranged = jnp.transpose(arranged, (1, 0, 2, 3)).reshape(key_heads, -1, HEAD_DIM)
    padded = jnp.pad(decode_entries, ((0, 0), (0, -decode_count % 16), (0, 0)))
    output, decoded = pl.pallas_call(
        attention_kernel,
        grid_spec=pltpu.PrefetchScalarGridSpec(
            num_scalar_prefetch=3,
            grid=(key_heads,),
            in_specs=[
                pl.BlockSpec((row_count, group * HEAD_DIM), lambda h, *_: (0, h)),
                pl.BlockSpec((1,) + arranged.shape[1:], lambda h, *_: (h, 0, 0)),
                pl.BlockSpec((2, row_count, HEAD_DIM), lambda h, *_: (0, 0, h)),
                pl.BlockSpec((2, padded.shape[1], HEAD_DIM), lambda h, *_: (0, 0, h)),
                pl.BlockSpec(memory_space=pl.ANY),
                pl.BlockSpec(memory_space=pl.ANY),
            ],
            out_specs=[
                pl.BlockSpec((row_count, group * HEAD_DIM), lambda h, *_: (0, h)),
                pl.BlockSpec((1,) + arranged.shape[1:], lambda h, *_: (h, 0, 0)),
            ],
            scratch_shapes=[
                pltpu.VMEM((page_count,) + pages.shape[1:], pages.dtype),
                pltpu.SemaphoreType.DMA,
            ],
        ),
        out_shape=[
            jax.ShapeDtypeStruct(queries.shape, jnp.bfloat16),
            jax.ShapeDtypeStruct(arranged.shape, jnp.bfloat16),
        ],
        compiler_params=pltpu.CompilerParams(
            dimension_semantics=("arbitrary",), vmem_limit_bytes=40 * 1024 * 1024
        ),
        name="paged_attention",
    )(places, prefix_length, context_length, queries, arranged, entries, padded, pages, own_pages)
    decoded = decoded.reshape(key_heads, decode_count, group, HEAD_DIM)
    decoded = jnp.transpose(decoded, (1, 0, 2, 3)).reshape(decode_queries.shape)
    return output, decoded


def exchange_kernel(chunks, shared, served, held, far_send, far_recv, side_send, side_recv, core_send,
                    core_recv):
    plane_count = served.shape[0]
    me = lax.axis_index("pool")
    plane = me // PLANE
    within = me % PLANE
    side = within // 2
    core = within % 2
    side_device = plane * PLANE + (1 - side) * 2 + core
    core_device = plane * PLANE + side * 2 + (1 - core)

    barrier = pltpu.get_barrier_semaphore()
    for offset in range(1, plane_count):
        pl.semaphore_signal(
            barrier, inc=1,
            device_id={"pool": lax.rem(plane + offset, plane_count) * PLANE + within},
            device_id_type=MESH,
        )
    for device in (side_device, core_device):
        pl.semaphore_signal(barrier, inc=1, device_id={"pool": device}, device_id_type=MESH)
    pl.semaphore_wait(barrier, plane_count + 1)

    def far(offset, k):
        target = lax.rem(plane + offset, plane_count)
        return pltpu.make_async_remote_copy(
            src_ref=served.at[target, pl.ds(*chunks[k])],
            dst_ref=held.at[me, pl.ds(*chunks[k])],
            send_sem=far_send.at[offset, k],
            recv_sem=far_recv.at[offset, k],
            device_id={"pool": target * PLANE + within},
            device_id_type=MESH,
        )

    def spread(offset, k, other_side, to_core):
        source_plane = lax.rem(plane + plane_count - offset, plane_count)
        row = (1 - side) if other_side else side
        source = source_plane * PLANE + row * 2 + core
        if offset == 0 and not other_side:
            block = served.at[plane, pl.ds(*chunks[k])]
        else:
            block = held.at[source, pl.ds(*chunks[k])]
        if to_core:
            send, recv = core_send.at[int(other_side), offset, k], core_recv.at[int(other_side), offset, k]
        else:
            send, recv = side_send.at[offset, k], side_recv.at[offset, k]
        return pltpu.make_async_remote_copy(
            src_ref=block,
            dst_ref=held.at[source, pl.ds(*chunks[k])],
            send_sem=send,
            recv_sem=recv,
            device_id={"pool": core_device if to_core else side_device},
            device_id_type=MESH,
        )

    count = len(chunks)
    for k in range(count):
        for offset in range(1, plane_count):
            far(offset, k).start()
    for k in range(count):
        if k < shared:
            spread(0, k, False, False).start()
        spread(0, k, False, True).start()

    def forward(k):
        for offset in range(plane_count):
            spread(offset, k, False, False).wait_recv()
            spread(offset, k, True, True).start()

    for k in range(count):
        for offset in range(1, plane_count):
            far(offset, k).wait_recv()
            if k < shared:
                spread(offset, k, False, False).start()
            spread(offset, k, False, True).start()
        if 0 < k <= shared:
            forward(k - 1)
    if shared == count:
        forward(count - 1)
    for k in range(count):
        for offset in range(plane_count):
            if offset:
                far(offset, k).wait_send()
            spread(offset, k, False, True).wait()
            if k < shared:
                spread(offset, k, False, False).wait_send()
                spread(offset, k, True, True).wait()


def exchange(served, shared_length, pool_size, collective_id):
    plane_count, length = served.shape[:2]
    shared_length = min(shared_length, length)
    shared = max(1, min(5, 20 // plane_count, shared_length))
    edges = [shared_length * k // shared for k in range(shared + 1)]
    if length > shared_length:
        middle = (length + shared_length) // 2
        edges += [middle, length] if middle > shared_length else [length]
    chunks = [(low, high - low) for low, high in zip(edges, edges[1:])]
    pieces = len(chunks)
    one = pltpu.SemaphoreType.DMA((plane_count, pieces))
    two = pltpu.SemaphoreType.DMA((2, plane_count, pieces))
    return pl.pallas_call(
        functools.partial(exchange_kernel, chunks, shared),
        out_shape=jax.ShapeDtypeStruct((pool_size,) + served.shape[1:], served.dtype),
        in_specs=[pl.BlockSpec(memory_space=pl.ANY)],
        out_specs=pl.BlockSpec(memory_space=pl.ANY),
        scratch_shapes=[one, one, one, one, two, two],
        compiler_params=pltpu.CompilerParams(
            collective_id=collective_id, has_side_effects=True
        ),
        name="page_exchange",
    )(served)


def gather_kernel(slots, pages, served, sem):
    target = pl.program_id(0)

    def fetch(t, carry):
        pltpu.make_async_copy(pages.at[slots[target, t]], served.at[0, t], sem).start()
        return carry

    lax.fori_loop(0, served.shape[1], fetch, 0)
    pltpu.make_async_copy(served, served, sem).wait()


def gather(slots, pages):
    block = (1, slots.shape[1]) + pages.shape[1:]
    return pl.pallas_call(
        gather_kernel,
        grid_spec=pltpu.PrefetchScalarGridSpec(
            num_scalar_prefetch=1,
            grid=slots.shape[:1],
            in_specs=[pl.BlockSpec(memory_space=pl.ANY)],
            out_specs=pl.BlockSpec(block, lambda q, *_: (q, 0, 0, 0, 0)),
            scratch_shapes=[pltpu.SemaphoreType.DMA],
        ),
        out_shape=jax.ShapeDtypeStruct(slots.shape + pages.shape[1:], pages.dtype),
        compiler_params=pltpu.CompilerParams(
            dimension_semantics=("arbitrary",), vmem_limit_bytes=24 * 1024 * 1024
        ),
        name="gather_pages",
    )(slots, pages)


def tables_kernel(table, tables, local_sem, part_send, part_recv, far_send, far_recv, near_send,
                  near_recv):
    parts, plane_count = tables.shape[1:3]
    part = lax.axis_index("replica")
    me = lax.axis_index("pool")
    plane = me // PLANE
    within = me % PLANE

    def other_part(offset):
        return {"replica": lax.rem(part + offset, parts), "pool": me}

    def other_plane(offset):
        return {"pool": lax.rem(plane + offset, plane_count) * PLANE + within}

    def other_place(offset):
        return {"pool": plane * PLANE + lax.rem(within + offset, PLANE)}

    barrier = pltpu.get_barrier_semaphore()
    stages = [(other_part, parts), (other_plane, plane_count), (other_place, PLANE)]
    for device_of, size in stages:
        for offset in range(1, size):
            pl.semaphore_signal(
                barrier, inc=1, device_id=device_of(offset), device_id_type=MESH
            )
    pl.semaphore_wait(barrier, parts + plane_count + PLANE - 3)
    mine = pltpu.make_async_copy(table, tables.at[within, part, plane], local_sem)
    mine.start()
    mine.wait()
    blocks = [
        tables.at[within, part, plane],
        tables.at[within, pl.ds(0, parts), plane],
        tables.at[within],
    ]
    sems = [(part_send, part_recv), (far_send, far_recv), (near_send, near_recv)]
    for (device_of, size), block, (send, recv) in zip(stages, blocks, sems):
        copies = [
            pltpu.make_async_remote_copy(
                src_ref=block,
                dst_ref=block,
                send_sem=send.at[offset],
                recv_sem=recv.at[offset],
                device_id=device_of(offset),
                device_id_type=MESH,
            )
            for offset in range(1, size)
        ]
        for copy in copies:
            copy.start()
        for copy in copies:
            copy.wait()


def gather_tables(named, parts, plane_count, collective_id):
    width = -(-named.shape[0] // 128) * 128
    table = jnp.pad(named, (0, width - named.shape[0]), constant_values=-1)[None, :]
    sems = [pltpu.SemaphoreType.DMA]
    for size in (parts, plane_count, PLANE):
        sems += [pltpu.SemaphoreType.DMA((size,))] * 2
    return pl.pallas_call(
        tables_kernel,
        out_shape=jax.ShapeDtypeStruct((PLANE, parts, plane_count, 1, width), jnp.int32),
        in_specs=[pl.BlockSpec(memory_space=pltpu.VMEM)],
        out_specs=pl.BlockSpec(memory_space=pltpu.VMEM),
        scratch_shapes=sems,
        compiler_params=pltpu.CompilerParams(
            collective_id=collective_id, has_side_effects=True
        ),
        name="gather_tables",
    )(table)


def on_device(
    stretch_queries,
    decode_queries,
    stretch_entries,
    decode_entries,
    pool_pages,
    page_owner,
    page_slot,
    prefix_length,
    context_length,
):
    pool_size = lax.axis_size("pool")
    parts = lax.axis_size("replica")
    part = lax.axis_index("replica")
    me = lax.axis_index("pool")
    plane_count = pool_size // PLANE
    page_count = page_slot.shape[0]
    slot_count, _, page_tokens, _ = pool_pages.shape
    capacity = max(2, 4 * page_count // (3 * pool_size))
    longest = min(slot_count, PLANE * capacity)

    first = jnp.concatenate(
        [jnp.arange(PRE_PAGES), jnp.tile(jnp.arange(DEC_PAGES), context_length.shape[0])]
    ).astype(jnp.int32) * page_tokens
    limit = jnp.concatenate(
        [
            jnp.broadcast_to(prefix_length, (PRE_PAGES,)),
            jnp.repeat(context_length, DEC_PAGES),
        ]
    )
    named = jnp.where(first < limit, page_owner[:, 0] * slot_count + page_slot, -1)
    everyone = gather_tables(named, parts, plane_count, 0)
    everyone = jnp.transpose(everyone, (1, 2, 0, 3, 4))
    everyone = everyone.reshape(parts * plane_count * 2, -1, 1)
    every_page = jnp.arange(pool_size * slot_count, dtype=jnp.int32)
    by_side = jnp.any(everyone == every_page, axis=1)
    by_side = by_side.reshape(parts, plane_count, 2, pool_size, slot_count)
    needed = (by_side[:, :, 0] | by_side[:, :, 1]).astype(jnp.int32)
    most = jnp.max(jnp.sum(needed, axis=-1))
    by_side = lax.dynamic_index_in_dim(by_side, part, 0, keepdims=False).astype(jnp.int32)
    source_side = (jnp.arange(pool_size)[:, None] // 2) % 2
    early = jnp.where(source_side == 0, by_side[:, 1], by_side[:, 0])
    late = jnp.maximum(by_side[:, 0], by_side[:, 1]) - early

    def ranked(early, late):
        early_rank = jnp.cumsum(early, axis=1) - 1
        late_rank = jnp.cumsum(late, axis=1) - 1 + jnp.sum(early, axis=1, keepdims=True)
        return jnp.where(early == 1, early_rank, jnp.where(late == 1, late_rank, -1))

    asked_rank = ranked(
        lax.dynamic_index_in_dim(early, me, 1, keepdims=False),
        lax.dynamic_index_in_dim(late, me, 1, keepdims=False),
    )
    plane = me // PLANE
    coming_rank = ranked(
        lax.dynamic_index_in_dim(early, plane, 0, keepdims=False),
        lax.dynamic_index_in_dim(late, plane, 0, keepdims=False),
    ).reshape(-1)
    rank = jnp.sum(
        jnp.where(named[:, None] == every_page[None, :], coming_rank[None, :], 0), axis=1
    )
    slot_index = jnp.arange(slot_count, dtype=jnp.int32)
    slots = jnp.sum(
        jnp.where(
            asked_rank[:, None, :] == jnp.arange(longest, dtype=jnp.int32)[None, :, None],
            slot_index[None, None, :],
            0,
        ),
        axis=2,
    )
    lengths = sorted({-(-longest * share // 32) for share in (20, 21, 22, 24, 32)})

    def finish(length, collective_id):
        served = gather(slots[:, :length], pool_pages)
        held = exchange(served, 2 * capacity, pool_size, collective_id)
        held = held.reshape((pool_size * length,) + pool_pages.shape[1:])
        owner = page_owner[:, 0]
        places = jnp.where(owner == me, -1 - page_slot, owner * length + rank)
        places = jnp.where(named >= 0, places, -1)
        return attention(
            places, prefix_length, context_length, stretch_queries, decode_queries,
            stretch_entries, decode_entries, held, pool_pages,
        )

    choice = sum((most > length).astype(jnp.int32) for length in lengths[:-1])
    return lax.switch(
        choice,
        [functools.partial(finish, length, index + 1) for index, length in enumerate(lengths)],
    )


def solution(mesh):
    rows = P(("replica", "pool"), None)
    entries = P(None, ("replica", "pool"), None)
    vector = P(("replica", "pool"))
    pages = P(("replica", "pool"), None, None, None)
    return jax.shard_map(
        on_device,
        mesh=mesh,
        in_specs=(rows, rows, entries, entries, pages, rows, vector, vector, vector),
        out_specs=(rows, rows),
        check_vma=False,
    )
```

profile of v0, /device:TPU:9, one launch (start us, length us, event | category | flops | bytes accessed | tf_op | source)
XLA Modules:
  0.0 203.1 jit_solution(7592960137988665851)
XLA Ops:
  0.6 0.7 broadcast_in_dim.65
  1.4 0.1 reshape.226
  1.5 0.1 tile.10
  2.2 0.8 compare_select_fusion.17
  3.0 0.5 pad_bitcast_fusion.table
  3.5 13.4 %gather_tables.1 = s32[4,2,4,1,128]{4,3,2,1,0:T(1,128)} custom-call(s32[1,128]{1,0:T(1,128)} %pad_bitcast_fusion.table), custom_call_target="tpu_custom_call" | custom-call | tf_op jit(solution)/shard_map/gather_tables/pallas_call | solution.py:368
  16.9 0.7 copy.103
  17.7 3.0 %fusion = pred[16,1024]{1,0:T(8,128)(4,1)S(1)} fusion(s32[16,256]{1,0:T(8,128)S(1)} %eq.124), kind=kLoop, calls=%fused_computation.71 | loop fusion | flops 8372224 | bytes 32768 | tf_op jit(solution)/shard_map/reduce_or | solution.py:416
  20.7 0.1 reshape.227
  20.9 0.1 maximum_subtract_fusion
  20.9 0.2 reduce_window_sum.34
  21.2 0.2 reduce_window_sum.35
  21.4 1.0 reduce_window_sum.36
  22.4 0.9 reduce_window_sum.37
  23.4 0.2 convert_reduce_fusion
  23.6 0.6 reduce_max.9
  26.9 176.3 %conditional.1 = (bf16[128,8192]{1,0:T(8,128)(2,1)}, bf16[4,8192]{1,0:T(4,128)(2,1)}) conditional(s32[]{:T(128)} %clamp.3, (s32[96]{0:T(128)S(1)}, s32[]{:T(128)}, s32[96,1]{0,1:T(1,128)}, s32[96]{0:T(128)}, s32[96]{0:T(128)S(1)}, /*index=5*/bf16[4,8192]{1,0:T(4,128)(2,1)}, bf16[2,4,1024]{2,1,0:T(4,128)(2,1)}, ...), branch_computations={%region_11.12_spmd.clone, %region_12.13_spmd.clone, %region_13.14_... | conditional | flops 330156 | bytes 45392440 | solution.py:466
  27.1 0.1 reduce_sum.84
  27.2 0.1 add_add_fusion.6
  27.3 0.1 add.184
  27.4 0.1 sub.92
  27.4 0.1 eq.246
  27.5 0.1 eq.249
  27.6 0.2 select_reduce_fusion.6
  27.8 0.7 compare_select_fusion.11.places
  28.5 0.2 reduce_sum.85
  28.7 0.1 compare_select_fusion.10
  28.7 0.2 select_reduce_fusion.7
  28.9 8.1 %gather_pages.8.served = bf16[4,24,2,16,1024]{4,3,2,1,0:T(8,128)(2,1)S(1)} custom-call(s32[4,24]{1,0:T(4,128)S(1)} %bitcast.188, bf16[64,2,16,1024]{3,2,1,0:T(8,128)(2,1)} %get-tuple-element.814.pages.own_pages), custom_call_target="tpu_custom_call" | custom-call | tf_op jit(solution)/shard_map/cond/branch_3_fun/gather_pages/pallas_call | solution.py:293
  37.0 0.0 copy-start.1
  37.0 2.7 %copy-done.1 = bf16[4,24,2,16,1024]{4,3,2,1,0:T(8,128)(2,1)} copy-done((bf16[4,24,2,16,1024]{4,3,2,1,0:T(8,128)(2,1)}, bf16[4,24,2,16,1024]{4,3,2,1,0:T(8,128)(2,1)S(1)}, u32[]{:S(2)}) %copy-start.1) | copy-done | bytes 6291480 | tf_op jit(solution)/shard_map/cond
  39.7 0.0 copy-start.18
  39.7 0.0 copy-start.23
  39.7 0.0 copy-start.8
  39.7 0.0 copy-start.13
  39.7 0.0 copy-start.28
  39.7 141.8 %page_exchange.8 = bf16[16,24,2,16,1024]{4,3,2,1,0:T(8,128)(2,1)} custom-call(bf16[4,24,2,16,1024]{4,3,2,1,0:T(8,128)(2,1)} %copy-done.1), custom_call_target="tpu_custom_call" | custom-call | tf_op jit(solution)/shard_map/cond/branch_3_fun/page_exchange/pallas_call | solution.py:267
  181.5 0.0 copy-done.18
  181.6 0.0 copy-done.23
  181.6 0.0 copy-done.8
  181.6 0.0 copy-done.13
  181.6 0.0 copy-done.28
  181.6 20.8 %paged_attention.8 = (bf16[128,8192]{1,0:T(8,128)(2,1)}, bf16[8,32,128]{2,1,0:T(8,128)(2,1)S(1)}) custom-call(s32[96]{0:T(128)S(1)} %compare_select_fusion.11.places, s32[1]{0:T(128)} %get-tuple-element.805.prefix_length, s32[4]{0:T(128)S(1)} %copy-done.28, bf16[128,8192]{1,0:T(8,128)(2,1)S(1)} %copy-done.8, ...), custom_call_target="tpu_custom_call" | custom-call | tf_op jit(solution)/shard_map/cond/branch_3_fun/paged_attention/pallas_call | solution.py:131
  202.5 0.7 copy.144
  (19 shorter events, 0.2 us)
Async XLA Ops:
  37.0 2.7 %copy-start.1 = (bf16[4,24,2,16,1024]{4,3,2,1,0:T(8,128)(2,1)}, bf16[4,24,2,16,1024]{4,3,2,1,0:T(8,128)(2,1)S(1)}, u32[]{:S(2)}) copy-start(bf16[4,24,2,16,1024]{4,3,2,1,0:T(8,128)(2,1)S(1)} %gather_pages.8.served) | copy-start | bytes 18874372 | tf_op jit(solution)/shard_map/cond
  39.7 141.8 %copy-start.18 = (bf16[4,8192]{1,0:T(4,128)(2,1)S(1)}, bf16[4,8192]{1,0:T(4,128)(2,1)}, u32[]{:S(2)}) copy-start(bf16[4,8192]{1,0:T(4,128)(2,1)} %get-tuple-element.811) | copy-start | bytes 196612 | tf_op jit(solution)/shard_map/cond
  39.7 141.9 %copy-start.23 = (bf16[2,4,1024]{2,1,0:T(4,128)(2,1)S(1)}, bf16[2,4,1024]{2,1,0:T(4,128)(2,1)}, u32[]{:S(2)}) copy-start(bf16[2,4,1024]{2,1,0:T(4,128)(2,1)} %get-tuple-element.812) | copy-start | bytes 49156 | tf_op jit(solution)/shard_map/cond
  39.7 141.9 %copy-start.8 = (bf16[128,8192]{1,0:T(8,128)(2,1)S(1)}, bf16[128,8192]{1,0:T(8,128)(2,1)}, u32[]{:S(2)}) copy-start(bf16[128,8192]{1,0:T(8,128)(2,1)} %get-tuple-element.815.queries) | copy-start | bytes 6291460 | tf_op jit(solution)/shard_map/cond
  39.7 141.9 %copy-start.13 = (bf16[2,128,1024]{2,1,0:T(8,128)(2,1)S(1)}, bf16[2,128,1024]{2,1,0:T(8,128)(2,1)}, u32[]{:S(2)}) copy-start(bf16[2,128,1024]{2,1,0:T(8,128)(2,1)} %get-tuple-element.816.entries) | copy-start | bytes 1572868 | tf_op jit(solution)/shard_map/cond
  39.7 141.9 %copy-start.28 = (s32[4]{0:T(128)S(1)}, s32[4]{0:T(128)}, u32[]{:S(2)}) copy-start(s32[4]{0:T(128)} %get-tuple-element.806.context_length) | copy-start | bytes 52 | tf_op jit(solution)/shard_map/cond
where the time goes:
time: 206 us; the launch traced here: 203 us
  Pallas kernels  184 us (89%)
  other arithmetic  8.58 us (4%)
  local copies, waits for them, and re-layouts  6.1 us (3%)
  between operations  4.01 us (2%)
    pallas_call x1, Pallas kernels, exchange(): pl.pallas_call(functools.partial(exchange_kernel, chunks, shared), out_sh...  142 us
    pallas_call x1, Pallas kernels, attention(): pl.pallas_call(attention_kernel, grid_spec=pltpu.PrefetchScalarGridSpec(n...  20.8 us
    pallas_call x1, Pallas kernels, gather_tables(): pl.pallas_call(tables_kernel, out_shape=jax.ShapeDtypeStruct((PLANE, part...  13.4 us
    pallas_call x1, Pallas kernels, gather(): pl.pallas_call(gather_kernel, grid_spec=pltpu.PrefetchScalarGridSpec(num_...  8.09 us

commit v1 on v0

--- a/solution.py
+++ b/solution.py
@@ -40,7 +40,7 @@
 def attention_kernel(
     places, prefix_length, context_length,
     queries, decode_queries, entries, decode_entries, pages, own_pages,
-    output, decode_output, cache, sem,
+    output, decode_output, cache, sems,
 ):
     page_count, _, page_tokens, _ = cache.shape
     head = pl.program_id(0)
@@ -49,7 +49,7 @@
 
     @pl.when(head == 0)
     def _():
-        def fetch(t, carry):
+        def fetch(sem, t, carry):
             place = places[t]
 
             @pl.when(place >= 0)
@@ -62,8 +62,10 @@
 
             return carry
 
-        lax.fori_loop(0, page_count, fetch, 0)
-        pltpu.make_async_copy(cache, cache, sem).wait()
+        lax.fori_loop(0, PRE_PAGES, functools.partial(fetch, sems.at[0]), 0)
+        lax.fori_loop(PRE_PAGES, page_count, functools.partial(fetch, sems.at[1]), 0)
+        prefix = cache.at[pl.ds(0, PRE_PAGES)]
+        pltpu.make_async_copy(prefix, prefix, sems.at[0]).wait()
 
     columns = pl.ds(pl.multiple_of(head * HEAD_DIM, HEAD_DIM), HEAD_DIM)
     span = PRE_PAGES * page_tokens
@@ -94,6 +96,11 @@
             output[:, (start + g) * HEAD_DIM : (start + g + 1) * HEAD_DIM] = result[
                 g * row_count : (g + 1) * row_count
             ]
+
+    @pl.when(head == 0)
+    def _():
+        context = cache.at[pl.ds(PRE_PAGES, page_count - PRE_PAGES)]
+        pltpu.make_async_copy(context, context, sems.at[1]).wait()
 
     context_span = (page_count - PRE_PAGES) * page_tokens
     row_span = DEC_PAGES * page_tokens
@@ -147,7 +154,7 @@
             ],
             scratch_shapes=[
                 pltpu.VMEM((page_count,) + pages.shape[1:], pages.dtype),
-                pltpu.SemaphoreType.DMA,
+                pltpu.SemaphoreType.DMA((2,)),
             ],
         ),
         out_shape=[
@@ -271,7 +278,8 @@
         out_specs=pl.BlockSpec(memory_space=pl.ANY),
         scratch_shapes=[one, one, one, one, two, two],
         compiler_params=pltpu.CompilerParams(
-            collective_id=collective_id, has_side_effects=True
+            collective_id=collective_id, has_side_effects=True,
+            vmem_limit_bytes=56 * 1024 * 1024,
         ),
         name="page_exchange",
     )(served)
@@ -301,7 +309,7 @@
         ),
         out_shape=jax.ShapeDtypeStruct(slots.shape + pages.shape[1:], pages.dtype),
         compiler_params=pltpu.CompilerParams(
-            dimension_semantics=("arbitrary",), vmem_limit_bytes=24 * 1024 * 1024
+            dimension_semantics=("arbitrary",), vmem_limit_bytes=56 * 1024 * 1024
         ),
         name="gather_pages",
     )(slots, pages)

time: 206 us -> 210 us (1.019)
  Pallas kernels: 184 us -> 191 us
  local copies, waits for them, and re-layouts: 6.1 us -> 3.41 us
    pallas_call x1, Pallas kernels: 20.8 us -> 25.6 us  [attention(): pl.pallas_call(attention_kernel, grid_spec=pltpu.PrefetchScalarGridSpec(n...]
    cond x14, local copies, waits for them, and re-layouts: 3.42 us -> 0.73 us
where the time goes in v1:
time: 210 us; the launch traced here: 208 us
  Pallas kernels  191 us (91%)
  other arithmetic  9.17 us (4%)
  between operations  4.01 us (2%)
  local copies, waits for them, and re-layouts  3.41 us (2%)
    pallas_call x1, Pallas kernels, exchange(): pl.pallas_call(functools.partial(exchange_kernel, chunks, shared), out_sh...  143 us
    pallas_call x1, Pallas kernels, attention(): pl.pallas_call(attention_kernel, grid_spec=pltpu.PrefetchScalarGridSpec(n...  25.6 us
    pallas_call x1, Pallas kernels, gather_tables(): pl.pallas_call(tables_kernel, out_shape=jax.ShapeDtypeStruct((PLANE, part...  13.4 us
    pallas_call x1, Pallas kernels, gather(): pl.pallas_call(gather_kernel, grid_spec=pltpu.PrefetchScalarGridSpec(num_...  9.78 us

profile of v1, /device:TPU:9, one launch (start us, length us, event | category | flops | bytes accessed | tf_op | source)
XLA Modules:
  0.0 208.3 jit_solution(7047306842187435748)
XLA Ops:
  0.6 0.7 broadcast_in_dim.65
  1.4 0.1 reshape.226
  1.5 0.1 tile.10
  2.2 0.8 compare_select_fusion.17
  3.0 0.5 pad_bitcast_fusion.table
  3.5 13.4 %gather_tables.1 = s32[4,2,4,1,128]{4,3,2,1,0:T(1,128)} custom-call(s32[1,128]{1,0:T(1,128)} %pad_bitcast_fusion.table), custom_call_target="tpu_custom_call" | custom-call | tf_op jit(solution)/shard_map/gather_tables/pallas_call | solution.py:376
  16.9 0.7 copy.103
  17.7 3.0 %fusion = pred[16,1024]{1,0:T(8,128)(4,1)S(1)} fusion(s32[16,256]{1,0:T(8,128)S(1)} %eq.124), kind=kLoop, calls=%fused_computation.71 | loop fusion | flops 8372224 | bytes 32768 | tf_op jit(solution)/shard_map/reduce_or | solution.py:424
  20.7 0.1 reshape.227
  20.9 0.1 maximum_subtract_fusion
  20.9 0.2 reduce_window_sum.34
  21.2 0.2 reduce_window_sum.35
  21.4 1.0 reduce_window_sum.36
  22.4 0.9 reduce_window_sum.37
  23.4 0.2 convert_reduce_fusion
  23.6 0.6 reduce_max.9
  26.9 181.5 %conditional.1 = (bf16[128,8192]{1,0:T(8,128)(2,1)}, bf16[4,8192]{1,0:T(4,128)(2,1)}) conditional(s32[]{:T(128)} %clamp.3, (s32[96]{0:T(128)S(1)}, s32[]{:T(128)}, s32[96,1]{0,1:T(1,128)}, s32[96]{0:T(128)}, s32[96]{0:T(128)S(1)}, /*index=5*/bf16[4,8192]{1,0:T(4,128)(2,1)}, bf16[2,4,1024]{2,1,0:T(4,128)(2,1)}, ...), branch_computations={%region_11.12_spmd.clone, %region_12.13_spmd.clone, %region_13.14_... | conditional | flops 330156 | bytes 28615226 | solution.py:474
  27.1 0.1 reduce_sum.84
  27.2 0.1 add_add_fusion.6
  27.3 0.1 add.184
  27.4 0.1 sub.92
  27.4 0.1 eq.246
  27.5 0.1 eq.249
  27.6 0.2 select_reduce_fusion.6
  27.8 0.7 compare_select_fusion.11.places
  28.5 0.2 reduce_sum.85
  28.7 0.1 compare_select_fusion.10
  28.7 0.7 select_reduce_fusion.7
  29.5 9.8 %gather_pages.8.served = bf16[4,24,2,16,1024]{4,3,2,1,0:T(8,128)(2,1)} custom-call(s32[4,24]{1,0:T(4,128)} %bitcast.211, bf16[64,2,16,1024]{3,2,1,0:T(8,128)(2,1)} %get-tuple-element.814.pages.own_pages), custom_call_target="tpu_custom_call" | custom-call | tf_op jit(solution)/shard_map/cond/branch_3_fun/gather_pages/pallas_call | solution.py:301
  39.3 0.0 copy-start.18
  39.3 0.0 copy-start.23
  39.3 0.0 copy-start.3
  39.3 0.0 copy-start.8
  39.3 0.0 copy-start.13
  39.3 0.0 copy-start.28
  39.3 142.5 %page_exchange.8 = bf16[16,24,2,16,1024]{4,3,2,1,0:T(8,128)(2,1)} custom-call(bf16[4,24,2,16,1024]{4,3,2,1,0:T(8,128)(2,1)} %gather_pages.8.served), custom_call_target="tpu_custom_call" | custom-call | tf_op jit(solution)/shard_map/cond/branch_3_fun/page_exchange/pallas_call | solution.py:274
  181.9 0.0 copy-done.18
  181.9 0.0 copy-done.23
  181.9 0.0 copy-done.3
  182.0 0.0 copy-done.8
  182.0 0.0 copy-done.13
  182.0 0.0 copy-done.28
  182.0 25.6 %paged_attention.8 = (bf16[128,8192]{1,0:T(8,128)(2,1)}, bf16[8,32,128]{2,1,0:T(8,128)(2,1)S(1)}) custom-call(s32[96]{0:T(128)S(1)} %compare_select_fusion.11.places, s32[1]{0:T(128)} %get-tuple-element.805.prefix_length, s32[4]{0:T(128)S(1)} %copy-done.28, bf16[128,8192]{1,0:T(8,128)(2,1)S(1)} %copy-done.8, ...), custom_call_target="tpu_custom_call" | custom-call | tf_op jit(solution)/shard_map/cond/branch_3_fun/paged_attention/pallas_call | solution.py:138
  207.7 0.7 copy.144
  (19 shorter events, 0.2 us)
Async XLA Ops:
  39.3 142.6 %copy-start.18 = (bf16[4,8192]{1,0:T(4,128)(2,1)S(1)}, bf16[4,8192]{1,0:T(4,128)(2,1)}, u32[]{:S(2)}) copy-start(bf16[4,8192]{1,0:T(4,128)(2,1)} %get-tuple-element.811) | copy-start | bytes 196612 | tf_op jit(solution)/shard_map/cond
  39.3 142.6 %copy-start.23 = (bf16[2,4,1024]{2,1,0:T(4,128)(2,1)S(1)}, bf16[2,4,1024]{2,1,0:T(4,128)(2,1)}, u32[]{:S(2)}) copy-start(bf16[2,4,1024]{2,1,0:T(4,128)(2,1)} %get-tuple-element.812) | copy-start | bytes 49156 | tf_op jit(solution)/shard_map/cond
  39.3 142.7 %copy-start.3 = (bf16[64,2,16,1024]{3,2,1,0:T(8,128)(2,1)S(1)}, bf16[64,2,16,1024]{3,2,1,0:T(8,128)(2,1)}, u32[]{:S(2)}) copy-start(bf16[64,2,16,1024]{3,2,1,0:T(8,128)(2,1)} %get-tuple-element.814.pages.own_pages) | copy-start | bytes 12582916 | tf_op jit(solution)/shard_map/cond
  39.3 142.7 %copy-start.8 = (bf16[128,8192]{1,0:T(8,128)(2,1)S(1)}, bf16[128,8192]{1,0:T(8,128)(2,1)}, u32[]{:S(2)}) copy-start(bf16[128,8192]{1,0:T(8,128)(2,1)} %get-tuple-element.815.queries) | copy-start | bytes 6291460 | tf_op jit(solution)/shard_map/cond
  39.3 142.7 %copy-start.13 = (bf16[2,128,1024]{2,1,0:T(8,128)(2,1)S(1)}, bf16[2,128,1024]{2,1,0:T(8,128)(2,1)}, u32[]{:S(2)}) copy-start(bf16[2,128,1024]{2,1,0:T(8,128)(2,1)} %get-tuple-element.816.entries) | copy-start | bytes 1572868 | tf_op jit(solution)/shard_map/cond
  39.3 142.6 %copy-start.28 = (s32[4]{0:T(128)S(1)}, s32[4]{0:T(128)}, u32[]{:S(2)}) copy-start(s32[4]{0:T(128)} %get-tuple-element.806.context_length) | copy-start | bytes 52 | tf_op jit(solution)/shard_map/cond
